TPU v7x, 32 devices: a whole 2x2x4 slice. The times are simulated.
32 devices in a mesh: fsdp: 2 (over x), ep: 16 (over z, y, core).
Axes of the slice: x: 2, y: 2, z: 4, core: 2. Of those that a mesh axis runs over, the one named last changes fastest.
Arguments:
- hidden_rows: bfloat16 [1024, 2, 4096], P('fsdp'), may hold values from -6 to 6
- norm_gain: float32 [4096], replicated, may hold values from 0.1 to 1.9
- route_expert: int32 [1024, 2, 2], P('fsdp'), may hold values from 0 to 3, all different within a row
- route_weight: float32 [1024, 2, 2], P('fsdp'), may hold values from 0.2 to 1
- gate_base: bfloat16 [16, 4096, 384], P('ep'), may hold values from -0.09375 to 0.09375
- up_base: bfloat16 [16, 4096, 384], P('ep'), may hold values from -0.09375 to 0.09375
- down_base: bfloat16 [16, 384, 4096], P('ep'), may hold values from -0.15625 to 0.15625
- tile_values: bfloat16 [1024, 128, 128], P(('fsdp', 'ep')), may hold values from -6 to 6
- tile_scale: float32 [1024], P(('fsdp', 'ep')), may hold values from 0.01 to 0.08
- tile_owner: int32 [1024, 1], P(('fsdp', 'ep')), may hold values from 0 to 15; in each aligned block of 32 rows (0 to 31, 32 to 63, ...) at most 4 rows name the same one
- tile_slot: int32 [1024], P(('fsdp', 'ep')), may hold values from 0 to 287
Outputs:
- layer_out: bfloat16 [1024, 2, 4096], P(('fsdp', 'ep'))
Inputs may be any that keep to these rules, and one draw needn't show every extreme that they name: `tile_owner`: among the 32 tiles of one trainer device no owner is named more than 4 times. `route_expert`: each row and step names 2 different experts.
All inputs are finite; a program needn't handle non-finite values.
Results may differ from a plain program's by a relative error of at most 0.022.
Values may be sent and summed in bfloat16 or wider, within the bound.
A program may use at most 256 MiB of HBM per device.

v0:
```python
import functools

import jax
import jax.numpy as jnp
from jax import lax
from jax.experimental import pallas as pl
from jax.experimental.pallas import tpu as pltpu
from jax.sharding import PartitionSpec as P

MESH = pl.DeviceIdType.MESH
EPSILON = 1e-06
CAP = 4
LANES = 128


def xor(value, constant, size):
    result = 0
    bit = 1
    while bit < size:
        result = result + lax.rem(lax.div(value, bit) + (constant // bit) % 2, 2) * bit
        bit *= 2
    return result


def partner(me, step, size):
    return xor(me, step, size)


def pack_kernel(owner_ref, slot_ref, scale_ref, tiles_ref, out_ref, slots_ref, count_ref):
    held = tiles_ref.shape[0]
    owners, cap = out_ref.shape[:2]

    @pl.loop(0, owners)
    def _(o):
        count_ref[o] = 0
        for k in range(cap):
            slots_ref[o, 0, k] = -1

    @pl.loop(0, held)
    def _(t):
        o = owner_ref[t]
        k = count_ref[o]
        count_ref[o] = k + 1
        slots_ref[o, 0, k] = slot_ref[t]
        out_ref[o, k] = (tiles_ref[t].astype(jnp.float32) * scale_ref[t]).astype(out_ref.dtype)


def pack(tiles, scale, owner, slot, owners):
    edge = tiles.shape[1]
    smem = pl.BlockSpec(memory_space=pltpu.SMEM)
    vmem = pl.BlockSpec(memory_space=pltpu.VMEM)
    return pl.pallas_call(
        pack_kernel,
        out_shape=(
            jax.ShapeDtypeStruct((owners, CAP, edge, edge), jnp.bfloat16),
            jax.ShapeDtypeStruct((owners, 1, LANES), jnp.int32),
        ),
        in_specs=[smem, smem, smem, vmem],
        out_specs=(vmem, smem),
        scratch_shapes=[pltpu.SMEM((owners,), jnp.int32)],
        compiler_params=pltpu.CompilerParams(vmem_limit_bytes=24 << 20),
        name="pack",
    )(owner, slot, scale, tiles)


def exchange_kernel(
    n,
    groups,
    tiles_ref,
    slots_ref,
    rows_ref,
    gain_ref,
    tiles_out,
    slots_out,
    normed_out,
    row_in,
    row_out,
    in_sem,
    out_sem,
    own_sem,
    tile_send,
    tile_recv,
    slot_send,
    slot_recv,
    fwd_send,
    fwd_recv,
    fslot_send,
    fslot_recv,
):
    f = lax.axis_index("fsdp")
    e = lax.axis_index("ep")
    far = n // 2
    near_steps = list(range(1, far))
    far_steps = list(range(far, n))
    steps = []
    while near_steps or far_steps:
        if far_steps:
            steps.append(far_steps.pop(0))
        if near_steps:
            steps.append(near_steps.pop(0))

    barrier = pltpu.get_barrier_semaphore()
    for k in steps:
        pl.semaphore_signal(
            barrier, inc=1, device_id=(f, partner(e, k, n)), device_id_type=MESH
        )
    for g in range(1, groups):
        pl.semaphore_signal(
            barrier, inc=1, device_id=(lax.rem(f + g, groups), e), device_id_type=MESH
        )
    chunk = row_in.shape[1]
    chunks = rows_ref.shape[0] // chunk

    def load(i):
        return pltpu.make_async_copy(
            rows_ref.at[pl.ds(i * chunk, chunk)], row_in.at[i % 2], in_sem.at[i % 2]
        )

    def store(i):
        steps_dim = rows_ref.shape[1]
        return pltpu.make_async_copy(
            row_out.at[i % 2],
            normed_out.at[pl.ds(i * chunk * steps_dim, chunk * steps_dim)],
            out_sem.at[i % 2],
        )

    load(0).start()
    pl.semaphore_wait(barrier, n - 1 + groups - 1)

    waits = []

    def remote(src, dst, send, recv, target):
        copy = pltpu.make_async_remote_copy(
            src_ref=src,
            dst_ref=dst,
            send_sem=send,
            recv_sem=recv,
            device_id=target,
            device_id_type=MESH,
        )
        copy.start()
        waits.append(copy)
        return copy

    def forward(tile_src, slot_src, k, source):
        copies = []
        for g in range(1, groups):
            target = (lax.rem(f + g, groups), e)
            copies.append(
                remote(slot_src, slots_out.at[f, source], fslot_send.at[g, k],
                       fslot_recv.at[g, k], target)
            )
            copies.append(
                remote(tile_src, tiles_out.at[f, source], fwd_send.at[g, k],
                       fwd_recv.at[g, k], target)
            )
        return copies

    arrivals = {}
    forwards = forward(tiles_ref.at[e], slots_ref.at[e], 0, e)
    for k in steps:
        to = partner(e, k, n)
        slot_copy = remote(slots_ref.at[to], slots_out.at[f, e], slot_send.at[k],
                           slot_recv.at[k], (f, to))
        tile_copy = remote(tiles_ref.at[to], tiles_out.at[f, e], tile_send.at[k],
                           tile_recv.at[k], (f, to))
        arrivals[k] = (slot_copy, tile_copy)
    own = (
        pltpu.make_async_copy(tiles_ref.at[e], tiles_out.at[f, e], own_sem.at[0]),
        pltpu.make_async_copy(slots_ref.at[e], slots_out.at[f, e], own_sem.at[1]),
    )
    for copy in own:
        copy.start()

    def normalise(i):
        if i + 1 < chunks:
            load(i + 1).start()
        load(i).wait()
        if i >= 2:
            store(i - 2).wait()
        group = 8

        @pl.loop(0, chunk // group)
        def _(j):
            block = row_in[i % 2, pl.ds(j * group, group)].astype(jnp.float32)
            values = block.reshape(group * block.shape[1], block.shape[2])
            scaled = values * lax.rsqrt(
                jnp.mean(values * values, axis=-1, keepdims=True) + EPSILON
            )
            first = pl.multiple_of(j * values.shape[0], values.shape[0])
            row_out[i % 2, pl.ds(first, values.shape[0])] = (scaled * gain_ref[...]).astype(
                row_out.dtype
            )

        store(i).start()

    for i in range(max(chunks, len(steps))):
        if i < chunks:
            normalise(i)
        if i < len(steps):
            k = steps[i]
            source = partner(e, k, n)
            slot_copy, tile_copy = arrivals[k]
            slot_copy.wait_recv()
            tile_copy.wait_recv()
            forwards += forward(
                tiles_out.at[f, source], slots_out.at[f, source], k, source
            )
    for i in range(max(0, chunks - 2), chunks):
        store(i).wait()
    for copy in own:
        copy.wait()
    for copy in forwards:
        copy.wait_recv()
    for copy in waits:
        copy.wait_send()


def exchange(send_tiles, send_slots, hidden_rows, gain, groups):
    n, cap, edge, _ = send_tiles.shape
    rows, steps, width = hidden_rows.shape
    chunk = rows // 16
    any_spec = pl.BlockSpec(memory_space=pl.ANY)
    dma = pltpu.SemaphoreType.DMA
    return pl.pallas_call(
        functools.partial(exchange_kernel, n, groups),
        out_shape=(
            jax.ShapeDtypeStruct((groups, n, cap, edge, edge), jnp.bfloat16),
            jax.ShapeDtypeStruct((groups, n, 1, LANES), jnp.int32),
            jax.ShapeDtypeStruct((rows * steps, width), jnp.bfloat16),
        ),
        in_specs=[any_spec, any_spec, any_spec, pl.BlockSpec(memory_space=pltpu.VMEM)],
        out_specs=(any_spec, any_spec, any_spec),
        scratch_shapes=[
            pltpu.VMEM((2, chunk, steps, width), jnp.bfloat16),
            pltpu.VMEM((2, chunk * steps, width), jnp.bfloat16),
            dma((2,)),
            dma((2,)),
            dma((2,)),
            dma((n,)),
            dma((n,)),
            dma((n,)),
            dma((n,)),
            dma((groups, n)),
            dma((groups, n)),
            dma((groups, n)),
            dma((groups, n)),
        ],
        compiler_params=pltpu.CompilerParams(
            collective_id=0, has_side_effects=True, vmem_limit_bytes=24 << 20
        ),
        name="exchange",
    )(send_tiles, send_slots, hidden_rows, gain.reshape(1, -1))


def expert_kernel(
    slots_ref,
    tiles_ref,
    normed_ref,
    combine_ref,
    gate_ref,
    up_ref,
    down_ref,
    hidden_ref,
    down_new,
    tiles,
    normed,
    weights,
    total,
    head,
    chain,
    sems,
):
    hid = gate_ref.shape[2]
    width = gate_ref.shape[1]
    edge = tiles.shape[1]
    col_blocks = hid // edge
    row_blocks = width // edge
    third = row_blocks * col_blocks
    sources = slots_ref.shape[0]
    copies = [
        pltpu.make_async_copy(tiles_ref, tiles, sems.at[0]),
        pltpu.make_async_copy(gate_ref.at[0], weights.at[:, pl.ds(0, hid)], sems.at[1]),
        pltpu.make_async_copy(up_ref.at[0], weights.at[:, pl.ds(hid, hid)], sems.at[2]),
        pltpu.make_async_copy(down_ref.at[0], down_new, sems.at[3]),
        pltpu.make_async_copy(normed_ref, normed, sems.at[4]),
    ]
    for copy in copies:
        copy.start()

    @pl.loop(0, 3 * third)
    def _(s):
        head[s] = -1

    @pl.loop(0, sources)
    def _(d):
        for k in range(CAP):
            s = slots_ref[d, 0, k]

            @pl.when(s >= 0)
            def _():
                chain[d * CAP + k] = head[s]
                head[s] = d * CAP + k

    for copy in copies[:4]:
        copy.wait()

    def apply(s, target, rows, cols):
        first = head[s]

        @pl.when(first >= 0)
        def _():
            total[...] = target[rows, cols].astype(jnp.float32) + tiles[first].astype(jnp.float32)

            def more(entry):
                total[...] += tiles[entry].astype(jnp.float32)
                return chain[entry]

            lax.while_loop(lambda entry: entry >= 0, more, chain[first])
            target[rows, cols] = total[...].astype(target.dtype)

    @pl.loop(0, row_blocks)
    def _(r):
        span = pl.ds(pl.multiple_of(r * edge, edge), edge)
        for c in range(col_blocks):
            apply(r * col_blocks + c, weights, span, pl.ds(c * edge, edge))
            apply(third + r * col_blocks + c, weights, span, pl.ds(hid + c * edge, edge))
            apply(2 * third + c * row_blocks + r, down_new, pl.ds(c * edge, edge), span)

    copies[4].wait()
    block = 256

    @pl.loop(0, normed.shape[0] // block)
    def _(m):
        rows = pl.ds(pl.multiple_of(m * block, block), block)
        both = jnp.dot(normed[rows, :], weights[...], preferred_element_type=jnp.float32)
        gate = both[:, :hid]
        hidden_ref[rows, :] = (jax.nn.silu(gate) * both[:, hid:] * combine_ref[rows, :]).astype(
            hidden_ref.dtype
        )


def expert_hidden(slots, tiles, normed, combine, gate_base, up_base, down_base):
    rows, width = normed.shape
    hid = gate_base.shape[2]
    slot_count = 3 * gate_base.shape[1] * hid // (tiles.shape[1] ** 2)
    any_spec = pl.BlockSpec(memory_space=pl.ANY)
    vmem = pl.BlockSpec(memory_space=pltpu.VMEM)
    return pl.pallas_call(
        expert_kernel,
        out_shape=(
            jax.ShapeDtypeStruct((rows, hid), jnp.bfloat16),
            jax.ShapeDtypeStruct((hid, width), jnp.bfloat16),
        ),
        in_specs=[
            pl.BlockSpec(memory_space=pltpu.SMEM),
            any_spec,
            any_spec,
            vmem,
            any_spec,
            any_spec,
            any_spec,
        ],
        out_specs=(vmem, vmem),
        scratch_shapes=[
            pltpu.VMEM(tiles.shape, jnp.bfloat16),
            pltpu.VMEM((rows, width), jnp.bfloat16),
            pltpu.VMEM((width, 2 * hid), jnp.bfloat16),
            pltpu.VMEM(tiles.shape[1:], jnp.float32),
            pltpu.SMEM((slot_count,), jnp.int32),
            pltpu.SMEM((tiles.shape[0],), jnp.int32),
            pltpu.SemaphoreType.DMA((5,)),
        ],
        compiler_params=pltpu.CompilerParams(vmem_limit_bytes=52 << 20),
        name="expert",
    )(slots, tiles, normed, combine, gate_base, up_base, down_base)


def reduce_kernel(
    planes,
    parts,
    hidden_ref,
    down_ref,
    out_ref,
    part,
    core_buf,
    side_buf,
    line_buf,
    last_buf,
    core_send,
    core_recv,
    side_send,
    side_recv,
    line_send,
    line_recv,
    last_recv,
):
    f = lax.axis_index("fsdp")
    e = lax.axis_index("ep")
    z, y, c = lax.div(e, 4), lax.rem(lax.div(e, 2), 2), lax.rem(e, 2)
    core_peer = (f, z * 4 + y * 2 + (1 - c))
    side_peer = (f, z * 4 + (1 - y) * 2 + c)
    above = (f, lax.rem(e + 4, planes * 4))
    below = (f, lax.rem(e + planes * 4 - 4, planes * 4))
    chunk = part.shape[3]
    width = down_ref.shape[1]
    wide = width // parts
    tile = min(512, wide)

    barrier = pltpu.get_barrier_semaphore()
    pl.semaphore_signal(barrier, inc=1, device_id=core_peer, device_id_type=MESH)
    pl.semaphore_signal(barrier, inc=1, device_id=side_peer, device_id_type=MESH)

    @pl.when(z < planes - 1)
    def _():
        pl.semaphore_signal(barrier, inc=1, device_id=above, device_id_type=MESH)

    @pl.when(z > 0)
    def _():
        pl.semaphore_signal(barrier, inc=1, device_id=below, device_id_type=MESH)

    neighbours = jnp.where(z > 0, 1, 0) + jnp.where(z < planes - 1, 1, 0)
    pl.semaphore_wait(barrier, 2 + neighbours)

    table = [
        sorted(range(planes), key=lambda p, v=v: (-abs(p - v), -p if v < planes / 2 else p))
        for v in range(planes)
    ]

    def plane_of(step):
        return sum(jnp.where(z == v, table[v][step], 0) for v in range(planes))

    def remote(src, dst, send, recv, target):
        return pltpu.make_async_remote_copy(
            src_ref=src,
            dst_ref=dst,
            send_sem=send,
            recv_sem=recv,
            device_id=target,
            device_id_type=MESH,
        )

    pieces = [(step, h) for step in range(planes) for h in range(parts)]

    def core_copy(p, b):
        step, h = pieces[p]
        zz = plane_of(step)
        cols = pl.ds(h * wide, wide)
        return remote(
            part.at[zz, b, 1 - c, :, cols],
            core_buf.at[zz, b, :, cols],
            core_send.at[zz, h, b],
            core_recv.at[zz, h, b],
            core_peer,
        )

    def side_copy(p):
        step, h = pieces[p]
        zz = plane_of(step)
        cols = pl.ds(h * wide, wide)
        return remote(
            part.at[zz, 1 - y, c, :, cols],
            side_buf.at[zz, :, cols],
            side_send.at[zz, h],
            side_recv.at[zz, h],
            side_peer,
        )

    def line_copy(zz, h, target):
        cols = pl.ds(h * wide, wide)
        return remote(
            part.at[zz, y, c, :, cols],
            line_buf.at[zz, :, cols],
            line_send.at[zz, h],
            line_recv.at[zz, h],
            target,
        )

    def last_copy(zz, h, target):
        cols = pl.ds(h * wide, wide)
        return remote(
            part.at[zz, y, c, :, cols],
            last_buf.at[:, cols],
            line_send.at[zz, h],
            last_recv.at[h],
            target,
        )

    def compute(p):
        step, h = pieces[p]
        zz = plane_of(step)
        rows = pl.ds(pl.multiple_of(zz * 4 * chunk, 4 * chunk), 4 * chunk)

        @pl.loop(0, wide // tile)
        def _(j):
            cols = pl.ds(pl.multiple_of(h * wide + j * tile, tile), tile)
            product = jnp.dot(
                hidden_ref[rows, :], down_ref[:, cols], preferred_element_type=jnp.float32
            ).astype(part.dtype)
            part[zz, :, :, :, cols] = product.reshape(2, 2, chunk, tile)

        for b in range(2):
            core_copy(p, b).start()

    def pair(p):
        step, h = pieces[p]
        zz = plane_of(step)
        cols = pl.ds(h * wide, wide)
        for b in range(2):
            core_copy(p, b).wait_recv()
        for b in (1 - y, y):
            part[zz, b, c, :, cols] = (
                part[zz, b, c, :, cols].astype(jnp.float32)
                + core_buf[zz, b, :, cols].astype(jnp.float32)
            ).astype(part.dtype)
            if b is not y:
                side_copy(p).start()

    def line(p):
        step, h = pieces[p]
        zz = plane_of(step)
        cols = pl.ds(h * wide, wide)
        side_copy(p).wait_recv()

        def own():
            return part[zz, y, c, :, cols].astype(jnp.float32) + side_buf[zz, :, cols].astype(
                jnp.float32
            )

        if step < planes - 1:
            inner = ((zz > z) & (z > 0)) | ((zz < z) & (z < planes - 1))

            @pl.when(inner)
            def _():
                line_copy(zz, h, above).wait_recv()
                part[zz, y, c, :, cols] = (
                    own() + line_buf[zz, :, cols].astype(jnp.float32)
                ).astype(part.dtype)

            @pl.when(jnp.logical_not(inner))
            def _():
                part[zz, y, c, :, cols] = own().astype(part.dtype)

            @pl.when(zz > z)
            def _():
                line_copy(zz, h, above).start()

            @pl.when(zz == z - 1)
            def _():
                last_copy(zz, h, below).start()

            @pl.when(zz < z - 1)
            def _():
                line_copy(zz, h, below).start()
        else:
            out_ref[:, cols] = own()

            @pl.when(z > 0)
            def _():
                line_copy(zz, h, above).wait_recv()
                out_ref[:, cols] += line_buf[zz, :, cols].astype(jnp.float32)

            @pl.when(z < planes - 1)
            def _():
                last_copy(zz, h, below).wait_recv()
                out_ref[:, cols] += last_buf[:, cols].astype(jnp.float32)

    lag = 2 * parts
    for p in range(len(pieces) + 1):
        if p < len(pieces):
            compute(p)
        if p >= 1:
            pair(p - 1)
        if p >= lag + 1:
            line(p - 1 - lag)
    for p in range(len(pieces) - lag, len(pieces)):
        line(p)

    for p, (step, h) in enumerate(pieces):
        for b in range(2):
            core_copy(p, b).wait_send()
        side_copy(p).wait_send()
        if step < planes - 1:
            line_copy(plane_of(step), h, above).wait_send()


def down_and_reduce(hidden, down_new, n):
    rows, hid = hidden.shape
    width = down_new.shape[1]
    planes = n // 4
    chunk = rows // n
    parts = 2
    vmem = pl.BlockSpec(memory_space=pltpu.VMEM)
    dma = pltpu.SemaphoreType.DMA
    buf = lambda *shape: pltpu.VMEM(shape, jnp.bfloat16)
    return pl.pallas_call(
        functools.partial(reduce_kernel, planes, parts),
        out_shape=jax.ShapeDtypeStruct((chunk, width), jnp.float32),
        in_specs=[vmem, vmem],
        out_specs=vmem,
        scratch_shapes=[
            buf(planes, 2, 2, chunk, width),
            buf(planes, 2, chunk, width),
            buf(planes, chunk, width),
            buf(planes, chunk, width),
            buf(chunk, width),
            dma((planes, parts, 2)),
            dma((planes, parts, 2)),
            dma((planes, parts)),
            dma((planes, parts)),
            dma((planes, parts)),
            dma((planes, parts)),
            dma((parts,)),
        ],
        compiler_params=pltpu.CompilerParams(
            collective_id=1, has_side_effects=True, vmem_limit_bytes=44 << 20
        ),
        name="reduce",
    )(hidden, down_new)


def body(
    tsplit,
    hidden_rows,
    norm_gain,
    route_expert,
    route_weight,
    gate_base,
    up_base,
    down_base,
    tile_values,
    tile_scale,
    tile_owner,
    tile_slot,
):
    n = lax.axis_size("ep")
    groups = lax.axis_size("fsdp")
    rows, steps, width = hidden_rows.shape
    edge = tile_values.shape[1]
    send_tiles, send_slots = pack(tile_values, tile_scale, tile_owner[:, 0], tile_slot, n)
    expert = lax.axis_index("ep") // tsplit
    combine = jnp.sum(jnp.where(route_expert == expert, route_weight, 0.0), axis=-1)
    tiles, slots, normed = exchange(send_tiles, send_slots, hidden_rows, norm_gain, groups)
    hidden, down_new = expert_hidden(
        slots.reshape(groups * n, 1, LANES),
        tiles.reshape(groups * n * CAP, edge, edge),
        normed,
        combine.reshape(-1, 1),
        gate_base,
        up_base,
        down_base,
    )
    out = down_and_reduce(hidden, down_new, n)
    return out.reshape(rows // n, steps, width).astype(jnp.bfloat16)


TSPLIT = 4


def solution(mesh):
    return jax.shard_map(
        functools.partial(body, TSPLIT),
        mesh=mesh,
        in_specs=(
            P("fsdp", None, None),
            P(),
            P("fsdp", None, None),
            P("fsdp", None, None),
            P("ep", None, None),
            P("ep", None, None),
            P("ep", None, None),
            P(("fsdp", "ep"), None, None),
            P(("fsdp", "ep")),
            P(("fsdp", "ep"), None),
            P(("fsdp", "ep")),
        ),
        out_specs=P(("fsdp", "ep"), None, None),
        check_vma=False,
    )
```

profile of v0, /device:TPU:0, one launch (start us, length us, event | category | flops | bytes accessed | tf_op | source)
XLA Modules:
  0.0 155.7 jit_solution(7542015679194209929)
XLA Ops:
  0.0 0.7 fusion
  0.7 0.1 copy.13
  0.9 0.2 reshape.18.combine_ref
  1.1 0.0 copy-start.4
  1.1 1.2 copy-done.4
  2.3 0.0 copy-start.6
  2.3 0.7 copy-done.6
  2.9 0.0 copy-start.7
  2.9 0.7 copy-done.7
  3.6 0.0 copy-start.8
  3.6 0.7 copy-done.8
  4.2 1.8 %pack.1 = (bf16[16,4,128,128]{3,2,1,0:T(8,128)(2,1)S(1)}, s32[16,1,128]{2,1,0:T(1,128)S(1)}) custom-call(s32[32]{0:T(128)S(1)} %bitcast.7, s32[32]{0:T(128)S(1)} %copy-done.7, f32[32]{0:T(128)S(1)} %copy-done.8, bf16[32,128,128]{2,1,0:T(8,128)(2,1)S(1)} %copy-done.4), custom_call_target="tpu_custom_call" | custom-call | tf_op jit(solution)/shard_map/pack/pallas_call | solution.py:52
  6.1 0.0 copy-start
  6.1 3.4 %copy-done = bf16[512,2,4096]{2,1,0:T(2,128)(2,1)S(1)} copy-done((bf16[512,2,4096]{2,1,0:T(2,128)(2,1)S(1)}, bf16[512,2,4096]{2,1,0:T(2,128)(2,1)}, u32[]{:S(2)}) %copy-start) | copy-done | bytes 8388632
  9.5 0.0 copy-start.5
  9.5 0.7 copy-done.5
  10.2 68.8 %exchange.1 = (bf16[2,16,4,128,128]{4,3,2,1,0:T(8,128)(2,1)S(1)}, s32[2,16,1,128]{3,2,1,0:T(1,128)S(1)}, bf16[1024,4096]{1,0:T(8,128)(2,1)S(1)}) custom-call(bf16[16,4,128,128]{3,2,1,0:T(8,128)(2,1)S(1)} %get-tuple-element.12.tiles_ref, s32[16,1,128]{2,1,0:T(1,128)S(1)} %get-tuple-element.13.slots_ref, bf16[512,2,4096]{2,1,0:T(2,128)(2,1)S(1)} %copy-done, ...), custom_call_target="tpu_custom_call" | custom-call | tf_op jit(solution)/shard_map/exchange/pallas_call | solution.py:225
  79.0 0.0 copy-start.1
  79.0 3.2 %copy-done.1 = bf16[1024,4096]{1,0:T(8,128)(2,1)} copy-done((bf16[1024,4096]{1,0:T(8,128)(2,1)}, bf16[1024,4096]{1,0:T(8,128)(2,1)S(1)}, u32[]{:S(2)}) %copy-start.1) | copy-done | bytes 8388632
  82.2 0.0 copy-start.2
  82.2 2.0 %copy-done.2 = bf16[2,16,4,128,128]{4,3,2,1,0:T(8,128)(2,1)} copy-done((bf16[2,16,4,128,128]{4,3,2,1,0:T(8,128)(2,1)}, bf16[2,16,4,128,128]{4,3,2,1,0:T(8,128)(2,1)S(1)}, u32[]{:S(2)}) %copy-start.2) | copy-done | bytes 4194328
  84.2 16.2 %expert.1 = (bf16[1024,384]{1,0:T(8,128)(2,1)S(1)}, bf16[384,4096]{1,0:T(8,128)(2,1)}) custom-call(s32[32,1,128]{2,1,0:T(1,128)S(1)} %bitcast.6, bf16[128,128,128]{2,1,0:T(8,128)(2,1)} %bitcast.4, bf16[1024,4096]{1,0:T(8,128)(2,1)} %copy-done.1, f32[1024,1]{1,0:T(8,128)S(1)} %reshape.18.combine_ref, bf16[1,4096,384]{2,1,0:T(8,128)(2,1)} %gate_ref.1, ...), custom_call_target="tpu_custom_call" | custom-call | tf_op jit(solution)/shard_map/expert/pallas_call | solution.py:349
  100.3 0.0 copy-start.3
  100.3 1.9 %copy-done.3 = bf16[384,4096]{1,0:T(8,128)(2,1)S(1)} copy-done((bf16[384,4096]{1,0:T(8,128)(2,1)S(1)}, bf16[384,4096]{1,0:T(8,128)(2,1)}, u32[]{:S(2)}) %copy-start.3) | copy-done | bytes 3145752
  102.2 52.2 %reduce.1 = f32[64,4096]{1,0:T(8,128)S(1)} custom-call(bf16[1024,384]{1,0:T(8,128)(2,1)S(1)} %get-tuple-element.17.hidden_ref, bf16[384,4096]{1,0:T(8,128)(2,1)S(1)} %copy-done.3), custom_call_target="tpu_custom_call" | custom-call | tf_op jit(solution)/shard_map/reduce/pallas_call | solution.py:596
  154.5 0.1 convert_element_type.6
  154.5 1.1 convert_element_type.7
Async XLA Ops:
  1.1 1.2 copy-start.4
  2.3 0.7 copy-start.6
  2.9 0.7 copy-start.7
  3.6 0.7 copy-start.8
  6.1 3.4 %copy-start = (bf16[512,2,4096]{2,1,0:T(2,128)(2,1)S(1)}, bf16[512,2,4096]{2,1,0:T(2,128)(2,1)}, u32[]{:S(2)}) copy-start(bf16[512,2,4096]{2,1,0:T(2,128)(2,1)} %rows_ref.1) | copy-start | bytes 25165828
  9.5 0.7 copy-start.5
  79.0 3.2 %copy-start.1 = (bf16[1024,4096]{1,0:T(8,128)(2,1)}, bf16[1024,4096]{1,0:T(8,128)(2,1)S(1)}, u32[]{:S(2)}) copy-start(bf16[1024,4096]{1,0:T(8,128)(2,1)S(1)} %get-tuple-element.16.normed_ref) | copy-start | bytes 25165828
  82.2 2.0 %copy-start.2 = (bf16[2,16,4,128,128]{4,3,2,1,0:T(8,128)(2,1)}, bf16[2,16,4,128,128]{4,3,2,1,0:T(8,128)(2,1)S(1)}, u32[]{:S(2)}) copy-start(bf16[2,16,4,128,128]{4,3,2,1,0:T(8,128)(2,1)S(1)} %get-tuple-element.15) | copy-start | bytes 12582916
  100.3 1.9 %copy-start.3 = (bf16[384,4096]{1,0:T(8,128)(2,1)S(1)}, bf16[384,4096]{1,0:T(8,128)(2,1)}, u32[]{:S(2)}) copy-start(bf16[384,4096]{1,0:T(8,128)(2,1)} %get-tuple-element.18.down_ref) | copy-start | bytes 9437188
where the time goes:
time: 156 us
  Pallas kernels  139 us (89%)
  local copies, waits for them, and re-layouts  15.8 us (10%)
    pallas_call x1, Pallas kernels, exchange(): pl.pallas_call(functools.partial(exchange_kernel, n, groups), out_shape=(...  68.8 us
    pallas_call x1, Pallas kernels, down_and_reduce(): pl.pallas_call(functools.partial(reduce_kernel, planes, parts), out_shape...  52.2 us
    pallas_call x1, Pallas kernels, expert_hidden(): pl.pallas_call(expert_kernel, out_shape=(jax.ShapeDtypeStruct((rows, hid)...  16.2 us
    unnamed x18, local copies, waits for them, and re-layouts  14.4 us

commit v1 on v0

--- a/solution.py
+++ b/solution.py
@@ -89,15 +89,7 @@
 ):
     f = lax.axis_index("fsdp")
     e = lax.axis_index("ep")
-    far = n // 2
-    near_steps = list(range(1, far))
-    far_steps = list(range(far, n))
-    steps = []
-    while near_steps or far_steps:
-        if far_steps:
-            steps.append(far_steps.pop(0))
-        if near_steps:
-            steps.append(near_steps.pop(0))
+    steps = list(range(1, n))
 
     barrier = pltpu.get_barrier_semaphore()
     for k in steps:
@@ -247,7 +239,7 @@
             dma((groups, n)),
         ],
         compiler_params=pltpu.CompilerParams(
-            collective_id=0, has_side_effects=True, vmem_limit_bytes=24 << 20
+            collective_id=0, has_side_effects=True, vmem_limit_bytes=60 << 20
         ),
         name="exchange",
     )(send_tiles, send_slots, hidden_rows, gain.reshape(1, -1))

time: 156 us -> 142 us (0.910)
  Pallas kernels: 139 us -> 131 us
  local copies, waits for them, and re-layouts: 15.8 us -> 9.12 us
    pallas_call x1, Pallas kernels: 68.8 us -> 60.7 us  [exchange(): pl.pallas_call(functools.partial(exchange_kernel, n, groups), out_shape=(...]
    unnamed x18 -> x16, local copies, waits for them, and re-layouts: 14.4 us -> 7.69 us
where the time goes in v1:
time: 142 us; the launch traced here: 141 us
  Pallas kernels  131 us (92%)
  local copies, waits for them, and re-layouts  9.12 us (6%)
    pallas_call x1, Pallas kernels, exchange(): pl.pallas_call(functools.partial(exchange_kernel, n, groups), out_shape=(...  60.7 us
    pallas_call x1, Pallas kernels, down_and_reduce(): pl.pallas_call(functools.partial(reduce_kernel, planes, parts), out_shape...  52 us
    pallas_call x1, Pallas kernels, expert_hidden(): pl.pallas_call(expert_kernel, out_shape=(jax.ShapeDtypeStruct((rows, hid)...  16.6 us
    unnamed x16, local copies, waits for them, and re-layouts  7.69 us

profile of v1, /device:TPU:0, one launch (start us, length us, event | category | flops | bytes accessed | tf_op | source)
XLA Modules:
  0.0 141.1 jit_solution(5548355469353455926)
XLA Ops:
  0.0 0.7 fusion
  0.7 0.1 copy.13
  0.9 0.2 reshape.18.combine_ref
  1.1 0.0 copy-start.2
  1.1 1.2 copy-done.2
  2.3 0.0 copy-start.5
  2.3 0.7 copy-done.5
  2.9 0.0 copy-start.6
  2.9 0.7 copy-done.6
  3.6 0.0 copy-start.7
  3.6 0.7 copy-done.7
  4.2 1.8 %pack.1 = (bf16[16,4,128,128]{3,2,1,0:T(8,128)(2,1)S(1)}, s32[16,1,128]{2,1,0:T(1,128)S(1)}) custom-call(s32[32]{0:T(128)S(1)} %bitcast.5, s32[32]{0:T(128)S(1)} %copy-done.6, f32[32]{0:T(128)S(1)} %copy-done.7, bf16[32,128,128]{2,1,0:T(8,128)(2,1)S(1)} %copy-done.2), custom_call_target="tpu_custom_call" | custom-call | tf_op jit(solution)/shard_map/pack/pallas_call | solution.py:52
  6.1 0.0 copy-start.1
  6.1 1.3 copy-done.1
  7.4 0.0 copy-start.4
  7.4 0.6 copy-done.4
  8.0 60.7 %exchange.1 = (bf16[2,16,4,128,128]{4,3,2,1,0:T(8,128)(2,1)}, s32[2,16,1,128]{3,2,1,0:T(1,128)}, bf16[1024,4096]{1,0:T(8,128)(2,1)}) custom-call(bf16[16,4,128,128]{3,2,1,0:T(8,128)(2,1)} %copy-done.1, s32[16,1,128]{2,1,0:T(1,128)} %copy-done.4, bf16[512,2,4096]{2,1,0:T(2,128)(2,1)} %rows_ref.1, f32[1,4096]{1,0:T(1,128)} %bitcast.7), custom_call_target="tpu_custom_call" | custom-call | tf_op jit(solution)/shard_map/exchange/pallas_call | solution.py:217
  68.7 0.0 copy-start.3
  68.7 0.7 copy-done.3
  69.4 16.6 %expert.1 = (bf16[1024,384]{1,0:T(8,128)(2,1)S(1)}, bf16[384,4096]{1,0:T(8,128)(2,1)}) custom-call(s32[32,1,128]{2,1,0:T(1,128)S(1)} %bitcast.4, bf16[128,128,128]{2,1,0:T(8,128)(2,1)} %bitcast.6, bf16[1024,4096]{1,0:T(8,128)(2,1)} %get-tuple-element.16.normed_ref, f32[1024,1]{1,0:T(8,128)S(1)} %reshape.18.combine_ref, bf16[1,4096,384]{2,1,0:T(8,128)(2,1)} %gate_ref.1, ...), custom_call_target="tpu_custom_call" | custom-call | tf_op jit(solution)/shard_map/expert/pallas_call | solution.py:341
  86.0 0.0 copy-start
  86.0 1.9 %copy-done = bf16[384,4096]{1,0:T(8,128)(2,1)S(1)} copy-done((bf16[384,4096]{1,0:T(8,128)(2,1)S(1)}, bf16[384,4096]{1,0:T(8,128)(2,1)}, u32[]{:S(2)}) %copy-start) | copy-done | bytes 3145752
  87.9 52.0 %reduce.1 = f32[64,4096]{1,0:T(8,128)S(1)} custom-call(bf16[1024,384]{1,0:T(8,128)(2,1)S(1)} %get-tuple-element.17.hidden_ref, bf16[384,4096]{1,0:T(8,128)(2,1)S(1)} %copy-done), custom_call_target="tpu_custom_call" | custom-call | tf_op jit(solution)/shard_map/reduce/pallas_call | solution.py:588
  139.9 0.1 convert_element_type.6
  139.9 1.1 convert_element_type.7
Async XLA Ops:
  1.1 1.2 copy-start.2
  2.3 0.7 copy-start.5
  2.9 0.7 copy-start.6
  3.6 0.7 copy-start.7
  6.1 1.3 copy-start.1
  7.4 0.6 copy-start.4
  68.7 0.7 copy-start.3
  86.0 1.9 %copy-start = (bf16[384,4096]{1,0:T(8,128)(2,1)S(1)}, bf16[384,4096]{1,0:T(8,128)(2,1)}, u32[]{:S(2)}) copy-start(bf16[384,4096]{1,0:T(8,128)(2,1)} %get-tuple-element.18.down_ref) | copy-start | bytes 9437188

commit v2 on v1

--- a/solution.py
+++ b/solution.py
@@ -581,7 +581,7 @@
     width = down_new.shape[1]
     planes = n // 4
     chunk = rows // n
-    parts = 2
+    parts = 4
     vmem = pl.BlockSpec(memory_space=pltpu.VMEM)
     dma = pltpu.SemaphoreType.DMA
     buf = lambda *shape: pltpu.VMEM(shape, jnp.bfloat16)

time: 142 us -> 141 us (level)
  no operation moved by 1% of the time
where the time goes in v2:
time: 141 us
  Pallas kernels  131 us (93%)
  local copies, waits for them, and re-layouts  9.12 us (6%)
    pallas_call x1, Pallas kernels, exchange(): pl.pallas_call(functools.partial(exchange_kernel, n, groups), out_shape=(...  60.7 us
    pallas_call x1, Pallas kernels, down_and_reduce(): pl.pallas_call(functools.partial(reduce_kernel, planes, parts), out_shape...  50.9 us
    pallas_call x1, Pallas kernels, expert_hidden(): pl.pallas_call(expert_kernel, out_shape=(jax.ShapeDtypeStruct((rows, hid)...  17.2 us
    unnamed x16, local copies, waits for them, and re-layouts  7.69 us

profile of v2, /device:TPU:0, one launch (start us, length us, event | category | flops | bytes accessed | tf_op | source)
XLA Modules:
  0.0 140.6 jit_solution(8187933494144678154)
XLA Ops:
  0.0 0.7 fusion
  0.7 0.1 copy.13
  0.9 0.2 reshape.18.combine_ref
  1.1 0.0 copy-start.2
  1.1 1.2 copy-done.2
  2.3 0.0 copy-start.5
  2.3 0.7 copy-done.5
  2.9 0.0 copy-start.6
  2.9 0.7 copy-done.6
  3.6 0.0 copy-start.7
  3.6 0.7 copy-done.7
  4.2 1.8 %pack.1 = (bf16[16,4,128,128]{3,2,1,0:T(8,128)(2,1)S(1)}, s32[16,1,128]{2,1,0:T(1,128)S(1)}) custom-call(s32[32]{0:T(128)S(1)} %bitcast.5, s32[32]{0:T(128)S(1)} %copy-done.6, f32[32]{0:T(128)S(1)} %copy-done.7, bf16[32,128,128]{2,1,0:T(8,128)(2,1)S(1)} %copy-done.2), custom_call_target="tpu_custom_call" | custom-call | tf_op jit(solution)/shard_map/pack/pallas_call | solution.py:52
  6.1 0.0 copy-start.1
  6.1 1.3 copy-done.1
  7.4 0.0 copy-start.4
  7.4 0.6 copy-done.4
  8.0 60.7 %exchange.1 = (bf16[2,16,4,128,128]{4,3,2,1,0:T(8,128)(2,1)}, s32[2,16,1,128]{3,2,1,0:T(1,128)}, bf16[1024,4096]{1,0:T(8,128)(2,1)}) custom-call(bf16[16,4,128,128]{3,2,1,0:T(8,128)(2,1)} %copy-done.1, s32[16,1,128]{2,1,0:T(1,128)} %copy-done.4, bf16[512,2,4096]{2,1,0:T(2,128)(2,1)} %rows_ref.1, f32[1,4096]{1,0:T(1,128)} %bitcast.7), custom_call_target="tpu_custom_call" | custom-call | tf_op jit(solution)/shard_map/exchange/pallas_call | solution.py:217
  68.7 0.0 copy-start.3
  68.7 0.7 copy-done.3
  69.4 17.2 %expert.1 = (bf16[1024,384]{1,0:T(8,128)(2,1)S(1)}, bf16[384,4096]{1,0:T(8,128)(2,1)}) custom-call(s32[32,1,128]{2,1,0:T(1,128)S(1)} %bitcast.4, bf16[128,128,128]{2,1,0:T(8,128)(2,1)} %bitcast.6, bf16[1024,4096]{1,0:T(8,128)(2,1)} %get-tuple-element.16.normed_ref, f32[1024,1]{1,0:T(8,128)S(1)} %reshape.18.combine_ref, bf16[1,4096,384]{2,1,0:T(8,128)(2,1)} %gate_ref.1, ...), custom_call_target="tpu_custom_call" | custom-call | tf_op jit(solution)/shard_map/expert/pallas_call | solution.py:341
  86.7 0.0 copy-start
  86.7 1.9 %copy-done = bf16[384,4096]{1,0:T(8,128)(2,1)S(1)} copy-done((bf16[384,4096]{1,0:T(8,128)(2,1)S(1)}, bf16[384,4096]{1,0:T(8,128)(2,1)}, u32[]{:S(2)}) %copy-start) | copy-done | bytes 3145752
  88.5 50.9 %reduce.1 = f32[64,4096]{1,0:T(8,128)S(1)} custom-call(bf16[1024,384]{1,0:T(8,128)(2,1)S(1)} %get-tuple-element.17.hidden_ref, bf16[384,4096]{1,0:T(8,128)(2,1)S(1)} %copy-done), custom_call_target="tpu_custom_call" | custom-call | tf_op jit(solution)/shard_map/reduce/pallas_call | solution.py:588
  139.4 0.1 convert_element_type.6
  139.5 1.1 convert_element_type.7
Async XLA Ops:
  1.1 1.2 copy-start.2
  2.3 0.7 copy-start.5
  2.9 0.7 copy-start.6
  3.6 0.7 copy-start.7
  6.1 1.3 copy-start.1
  7.4 0.6 copy-start.4
  68.7 0.7 copy-start.3
  86.7 1.9 %copy-start = (bf16[384,4096]{1,0:T(8,128)(2,1)S(1)}, bf16[384,4096]{1,0:T(8,128)(2,1)}, u32[]{:S(2)}) copy-start(bf16[384,4096]{1,0:T(8,128)(2,1)} %get-tuple-element.18.down_ref) | copy-start | bytes 9437188
